TPU v7x, 32 devices: a whole 2x2x4 slice. The times are simulated.
32 devices in a mesh: dp: 2 (over x), seq: 16 (over z, y, core).
Axes of the slice: x: 2, y: 2, z: 4, core: 2. Of those that a mesh axis runs over, the one named last changes fastest.
Arguments:
- tokens: bfloat16 [2, 32, 256, 768], P('dp', 'seq'), may hold values from -6 to 6
- upstream: bfloat16 [2, 32, 256, 768], P('dp', 'seq'), may hold values from -0.15625 to 0.15625
- row_factor: bfloat16 [32, 256, 256], P('seq'), may hold values from -0.375 to 0.375
- column_factor: bfloat16 [256, 32, 32], P('seq'), may hold values from -1 to 1
Outputs:
- grad_row: bfloat16 [32, 256, 256], P('seq')
- grad_column: bfloat16 [256, 32, 32], P('seq')
All inputs are finite; a program needn't handle non-finite values.
Results may differ from a plain program's by a relative error of at most 0.005.
Values may be sent and summed in bfloat16 or wider, within the bound.
A program may use at most 64 MiB of HBM per device.

v0:
```python
import jax
import jax.numpy as jnp
from jax import lax
from jax.sharding import PartitionSpec as P


def apply_rows(row_factor, tokens):
    return jnp.einsum(
        "rij,brjd->brid", row_factor, tokens, preferred_element_type=jnp.float32
    ).astype(jnp.bfloat16)


def shards(tokens, upstream, row_factor, column_factor):
    mixed = apply_rows(row_factor, tokens)
    mixed_cols, upstream_cols = (
        lax.all_to_all(mixed, "seq", split_axis=2, concat_axis=1, tiled=True),
        lax.all_to_all(upstream, "seq", split_axis=2, concat_axis=1, tiled=True),
    )
    sum_column = jnp.einsum(
        "brcd,bscd->crs", upstream_cols, mixed_cols, preferred_element_type=jnp.float32
    )
    back_cols = jnp.einsum(
        "crs,brcd->bscd", column_factor, upstream_cols, preferred_element_type=jnp.float32
    ).astype(jnp.bfloat16)
    back_rows = lax.all_to_all(back_cols, "seq", split_axis=1, concat_axis=2, tiled=True)
    sum_row = jnp.einsum("brid,brjd->rij", back_rows, tokens, preferred_element_type=jnp.float32)
    total_row, total_column = lax.psum((sum_row, sum_column), "dp")
    return (total_row.astype(jnp.bfloat16), total_column.astype(jnp.bfloat16))


def solution(mesh):
    placed = (
        P("dp", "seq", None, None),
        P("dp", "seq", None, None),
        P("seq", None, None),
        P("seq", None, None),
    )
    return jax.shard_map(
        shards,
        mesh=mesh,
        in_specs=placed,
        out_specs=(P("seq", None, None), P("seq", None, None)),
        check_vma=False,
    )
```

profile of v0, /device:TPU:0, one launch (start us, length us, event | category | flops | bytes accessed | tf_op | source)
XLA Modules:
  0.0 103.7 jit_solution(1185870375113978503)
XLA Ops:
  0.6 0.0 copy-start
  0.6 2.9 %copy.19 = bf16[1,2,256,768]{3,1,0,2:T(2,128)(2,1)} copy(bf16[1,2,256,768]{3,2,1,0:T(8,128)(2,1)} %param.5) | data formatting | bytes 1572864 | tf_op args[1]
  3.5 0.0 copy-start.1
  3.5 7.5 %all-to-all-start = ((bf16[1,2,256,768]{3,1,0,2:T(2,128)(2,1)}), bf16[1,2,256,768]{3,1,0,2:T(2,128)(2,1)S(1)}, u32[]{:S(2)}, u32[]{:S(2)}) async-start(bf16[1,2,256,768]{3,1,0,2:T(2,128)(2,1)} %copy.19), calls=%async_computation | async-start | bytes 1572864 | tf_op jit(solution)/shard_map/all_to_all | solution.py:17
  11.1 0.0 copy-done
  11.1 0.0 copy-done.1
  11.1 0.4 fusion.1
  11.5 1.9 %copy.25 = bf16[1,2,256,768]{3,1,0,2:T(2,128)(2,1)} copy(bf16[1,2,256,768]{2,3,1,0:T(8,128)(2,1)S(1)} %fusion.1) | data formatting | bytes 1572864 | tf_op jit(solution)/shard_map/convert_element_type | solution.py:10
  13.4 16.4 %all-to-all-done = bf16[1,2,256,768]{3,1,0,2:T(2,128)(2,1)S(1)} async-done(((bf16[1,2,256,768]{3,1,0,2:T(2,128)(2,1)}), bf16[1,2,256,768]{3,1,0,2:T(2,128)(2,1)S(1)}, u32[]{:S(2)}, u32[]{:S(2)}) %all-to-all-start) | async-done | bytes 786464 | tf_op jit(solution)/shard_map/all_to_all | solution.py:17
  29.8 5.5 %all-to-all-start.2 = ((bf16[1,2,256,768]{3,1,0,2:T(2,128)(2,1)}), bf16[1,2,256,768]{3,1,0,2:T(2,128)(2,1)S(1)}, u32[]{:S(2)}, u32[]{:S(2)}) async-start(bf16[1,2,256,768]{3,1,0,2:T(2,128)(2,1)} %copy.25), calls=%async_computation.2 | async-start | bytes 1572864 | tf_op jit(solution)/shard_map/all_to_all | solution.py:16
  35.3 0.7 copy.32
  36.0 0.0 copy-start.2
  36.0 0.3 reshape.26
  36.3 0.6 copy-done.2
  36.9 0.4 fusion
  37.3 1.3 %copy.22 = bf16[1,32,16,768]{3,2,0,1:T(8,128)(2,1)} copy(bf16[1,32,16,768]{3,1,2,0:T(8,128)(2,1)S(1)} %fusion) | data formatting | bytes 1572864 | tf_op jit(solution)/shard_map/convert_element_type | solution.py:24
  38.6 15.3 %all-to-all-done.2 = bf16[1,2,256,768]{3,1,0,2:T(2,128)(2,1)S(1)} async-done(((bf16[1,2,256,768]{3,1,0,2:T(2,128)(2,1)}), bf16[1,2,256,768]{3,1,0,2:T(2,128)(2,1)S(1)}, u32[]{:S(2)}, u32[]{:S(2)}) %all-to-all-start.2) | async-done | bytes 786464 | tf_op jit(solution)/shard_map/all_to_all | solution.py:16
  54.0 5.5 %all-to-all-start.1 = ((bf16[1,32,16,768]{3,2,0,1:T(8,128)(2,1)}), bf16[1,32,16,768]{3,2,0,1:T(8,128)(2,1)S(1)}, u32[]{:S(2)}, u32[]{:S(2)}) async-start(bf16[1,32,16,768]{3,2,0,1:T(8,128)(2,1)} %copy.22), calls=%async_computation.1 | async-start | bytes 1572864 | tf_op jit(solution)/shard_map/all_to_all | solution.py:25
  59.5 0.1 copy.26
  59.5 1.7 %copy.27 = bf16[1,16,2,16,768]{4,2,1,3,0:T(2,128)(2,1)} copy(bf16[1,16,2,16,768]{4,3,1,2,0:T(8,128)(2,1)S(1)} %bitcast.39) | data formatting | bytes 1572864 | tf_op jit(solution)/shard_map/all_to_all | solution.py:16
  61.3 2.3 %reshape.29 = bf16[32,16,768]{2,0,1:T(8,128)(2,1)S(1)} reshape(bf16[1,16,2,16,768]{4,2,1,3,0:T(2,128)(2,1)} %copy.27) | data formatting | bytes 1572864 | tf_op jit(solution)/shard_map/reshape.9
  63.5 0.3 convolution_bitcast_fusion
  63.9 14.3 %all-to-all-done.1 = bf16[1,32,16,768]{3,2,0,1:T(8,128)(2,1)S(1)} async-done(((bf16[1,32,16,768]{3,2,0,1:T(8,128)(2,1)}), bf16[1,32,16,768]{3,2,0,1:T(8,128)(2,1)S(1)}, u32[]{:S(2)}, u32[]{:S(2)}) %all-to-all-start.1) | async-done | bytes 786464 | tf_op jit(solution)/shard_map/all_to_all | solution.py:25
  78.2 0.1 copy.23
  78.2 0.4 fusion.3
  78.6 24.3 %all-reduce.2 = (bf16[2,256,256]{2,1,0:T(8,128)(2,1)}, bf16[16,32,32]{1,2,0:T(8,128)(2,1)S(1)}) all-reduce(f32[2,256,256]{2,1,0:T(8,128)S(1)} %fusion.3, f32[16,32,32]{1,2,0:T(8,128)S(1)} %convolution_bitcast_fusion), channel_id=1, replica_groups=mesh['dp'=2,'seq'=16] {'dp'}, use_global_device_ids=true, to_apply=%region_0.0 | all-reduce | flops 147456 | bytes 884736 | tf_op jit(solution)/shard_map/psum | solution.py:27
  102.9 0.8 copy.28
Async XLA Ops:
  0.6 10.4 %copy-start = (bf16[1,2,256,768]{3,2,1,0:T(8,128)(2,1)S(1)}, bf16[1,2,256,768]{3,2,1,0:T(8,128)(2,1)}, u32[]{:S(2)}) copy-start(bf16[1,2,256,768]{3,2,1,0:T(8,128)(2,1)} %param.4) | copy-start | bytes 2359300
  3.5 7.5 %copy-start.1 = (bf16[2,256,256]{2,1,0:T(8,128)(2,1)S(1)}, bf16[2,256,256]{2,1,0:T(8,128)(2,1)}, u32[]{:S(2)}) copy-start(bf16[2,256,256]{2,1,0:T(8,128)(2,1)} %param.6) | copy-start | bytes 786436
  3.5 26.2 %all-to-all-start = ((bf16[1,2,256,768]{3,1,0,2:T(2,128)(2,1)}), bf16[1,2,256,768]{3,1,0,2:T(2,128)(2,1)S(1)}, u32[]{:S(2)}, u32[]{:S(2)}) async-start(bf16[1,2,256,768]{3,1,0,2:T(2,128)(2,1)} %copy.19), calls=%async_computation | async-start | bytes 1572864 | tf_op jit(solution)/shard_map/all_to_all | solution.py:17
  29.8 24.2 %all-to-all-start.2 = ((bf16[1,2,256,768]{3,1,0,2:T(2,128)(2,1)}), bf16[1,2,256,768]{3,1,0,2:T(2,128)(2,1)S(1)}, u32[]{:S(2)}, u32[]{:S(2)}) async-start(bf16[1,2,256,768]{3,1,0,2:T(2,128)(2,1)} %copy.25), calls=%async_computation.2 | async-start | bytes 1572864 | tf_op jit(solution)/shard_map/all_to_all | solution.py:16
  36.0 0.9 copy-start.2
  54.0 24.2 %all-to-all-start.1 = ((bf16[1,32,16,768]{3,2,0,1:T(8,128)(2,1)}), bf16[1,32,16,768]{3,2,0,1:T(8,128)(2,1)S(1)}, u32[]{:S(2)}, u32[]{:S(2)}) async-start(bf16[1,32,16,768]{3,2,0,1:T(8,128)(2,1)} %copy.22), calls=%async_computation.1 | async-start | bytes 1572864 | tf_op jit(solution)/shard_map/all_to_all | solution.py:25
where the time goes:
time: 104 us
  waiting for transfers between devices  46 us (44%)
  blocking collectives  24.3 us (23%)
  starting transfers between devices  18.5 us (18%)
  local copies, waits for them, and re-layouts  12.6 us (12%)
  matrix products  1.58 us (2%)
    psum x1, blocking collectives, shards(): total_row, total_column = lax.psum((sum_row, sum_column), 'dp')  24.3 us
    all_to_all x1, waiting for transfers between devices, shards(): lax.all_to_all(upstream, 'seq', split_axis=2, concat_axis=1, tiled=True)  16.4 us
    all_to_all x1, waiting for transfers between devices, shards(): lax.all_to_all(mixed, 'seq', split_axis=2, concat_axis=1, tiled=True)  15.3 us
    all_to_all x1, waiting for transfers between devices, shards(): lax.all_to_all(back_cols, 'seq', split_axis=1, concat_axis=2, tiled=True)  14.3 us
    all_to_all x1, starting transfers between devices, shards(): lax.all_to_all(upstream, 'seq', split_axis=2, concat_axis=1, tiled=True)  7.52 us
    all_to_all x1, starting transfers between devices, shards(): lax.all_to_all(mixed, 'seq', split_axis=2, concat_axis=1, tiled=True)  5.48 us
    all_to_all x1, starting transfers between devices, shards(): lax.all_to_all(back_cols, 'seq', split_axis=1, concat_axis=2, tiled=True)  5.48 us
    unnamed x8, local copies, waits for them, and re-layouts  4.27 us
  transfers between devices with their start and end apart: 3, of which 3 were waited for; matrix products, arithmetic and copies ran while one was open for 9% of the time, Pallas kernels for 0%

commit v1 on v0

v1 whole, which is shorter than its diff:
```python
import functools

import jax
import jax.numpy as jnp
from jax import lax
from jax.experimental import pallas as pl
from jax.experimental.pallas import tpu as pltpu
from jax.sharding import PartitionSpec as P

F32, BF16 = jnp.float32, jnp.bfloat16


def apply_rows(row_factor, tokens):
    return jnp.einsum(
        "rij,brjd->brid", row_factor, tokens, preferred_element_type=F32
    ).astype(BF16)


def plain_shards(tokens, upstream, row_factor, column_factor):
    mixed = apply_rows(row_factor, tokens)
    mixed_cols, upstream_cols = (
        lax.all_to_all(mixed, "seq", split_axis=2, concat_axis=1, tiled=True),
        lax.all_to_all(upstream, "seq", split_axis=2, concat_axis=1, tiled=True),
    )
    sum_column = jnp.einsum(
        "brcd,bscd->crs", upstream_cols, mixed_cols, preferred_element_type=F32
    )
    back_cols = jnp.einsum(
        "crs,brcd->bscd", column_factor, upstream_cols, preferred_element_type=F32
    ).astype(BF16)
    back_rows = lax.all_to_all(back_cols, "seq", split_axis=1, concat_axis=2, tiled=True)
    sum_row = jnp.einsum("brid,brjd->rij", back_rows, tokens, preferred_element_type=F32)
    total_row, total_column = lax.psum((sum_row, sum_column), "dp")
    return (total_row.astype(BF16), total_column.astype(BF16))


def dot(a, b, ca=1, cb=0):
    return lax.dot_general(a, b, (((ca,), (cb,)), ((), ())), preferred_element_type=F32)


def kernel(n, group, tok, up, rf, cf, grow, gcol,
           U, M, mloc, bloc, B, kmat, prow, precv, pcol, pcolr,
           su, ru, sm, rm, sb, rb, sr, rr, sc, rc):
    me = lax.axis_index("seq")
    other = 1 - lax.axis_index("dp")
    rows, C, D = up.shape
    cols = C // n
    R = rows * n
    lc, lr = cols.bit_length() - 1, R.bit_length() - 1
    full = R * cols
    groups = n // group

    def at(p, width=cols):
        return pl.ds(pl.multiple_of(p * width, width), width)

    def peer_of(k):
        return lax.rem(me + k, n)

    def remote(src, dst, send, recv, p):
        return pltpu.make_async_remote_copy(
            src_ref=src, dst_ref=dst, send_sem=send, recv_sem=recv,
            device_id={"seq": p}, device_id_type=pl.DeviceIdType.MESH)

    def across(src, dst, send, recv):
        return pltpu.make_async_remote_copy(
            src_ref=src, dst_ref=dst, send_sem=send, recv_sem=recv,
            device_id={"dp": other}, device_id_type=pl.DeviceIdType.MESH)

    def each_peer(body):
        @pl.loop(1, n)
        def _(k):
            body(peer_of(k))

    barrier = pltpu.get_barrier_semaphore()
    each_peer(lambda p: pl.semaphore_signal(
        barrier, inc=1, device_id={"seq": p}, device_id_type=pl.DeviceIdType.MESH))
    pl.semaphore_signal(barrier, inc=1, device_id={"dp": other}, device_id_type=pl.DeviceIdType.MESH)
    pl.semaphore_wait(barrier, n)

    each_peer(lambda p: remote(up.at[:, at(p), :], U.at[me], su.at[p], ru.at[me], p).start())
    U[me] = up[:, at(me), :]

    for r in range(rows):
        for h in range(0, D, 256):
            mloc[r, :, h:h + 256] = dot(rf[r], tok[r, :, h:h + 256]).astype(BF16)
    each_peer(lambda p: remote(mloc.at[:, at(p), :], M.at[me], sm.at[p], rm.at[me], p).start())
    M[me] = mloc[:, at(me), :]

    def iota(shape, dim):
        return lax.broadcasted_iota(jnp.int32, shape, dim)

    i, j = iota((full, full), 0), iota((full, full), 1)
    perm = (((i >> lr) == (j & (cols - 1))) & ((i & (R - 1)) == (j >> lc))).astype(F32).astype(BF16)
    spread = ((iota((full, R), 0) >> lc) == iota((full, R), 1)).astype(F32).astype(BF16)
    same = (i & (cols - 1)) == (j & (cols - 1))
    turned = dot(cf[...], perm, 0, 0).astype(BF16)
    kmat[...] = jnp.where(same, dot(spread, turned), 0.0).astype(BF16)

    each_peer(lambda p: remote(up.at[:, at(p), :], U.at[p], su.at[p], ru.at[p], p).wait_recv())
    for h in range(0, D, 256):
        flat = U[:, :, :, h:h + 256].reshape(full, 256)
        bloc[:, :, :, h:h + 256] = dot(kmat[...], flat).astype(BF16).reshape(n, rows, cols, 256)
    each_peer(lambda p: remote(bloc.at[p], B.at[me], sb.at[p], rb.at[me], p).start())
    B[me] = bloc[me]

    each_peer(lambda p: remote(mloc.at[:, at(p), :], M.at[p], sm.at[p], rm.at[p], p).wait_recv())
    pairs = dot(M[...].reshape(full, D), U[...].reshape(full, D), 1, 1)
    pairs = jnp.where(same, pairs, 0.0)
    high = pairs.astype(BF16)
    low = pairs - high.astype(F32)
    mid = low.astype(BF16)
    rest = (low - mid.astype(F32)).astype(BF16)
    pcol[...] = dot(spread, high, 0, 0) + dot(spread, mid, 0, 0) + dot(spread, rest, 0, 0)
    col_copy = across(pcol, pcolr, sc, rc)
    col_copy.start()

    def row_copy(g):
        part = at(g, group * cols)
        return across(prow.at[:, part, :], precv.at[:, part, :], sr.at[g], rr.at[g])

    first = lax.div(me, group)

    @pl.loop(0, groups)
    def _(k):
        g = lax.rem(first + k, groups)

        @pl.loop(0, group)
        def _(q):
            p = g * group + q

            @pl.when(p != me)
            def _():
                remote(bloc.at[p], B.at[p], sb.at[p], rb.at[p], p).wait_recv()

        part = at(g, group * cols)
        for r in range(rows):
            block = B[pl.ds(g * group, group), r].reshape(group * cols, D)
            prow[r, part, :] = dot(block, tok[r], 1, 1)
        row_copy(g).start()

    col_copy.wait()
    total = (pcol[...] + pcolr[...]).astype(BF16)
    gcol[...] = dot(perm, total, 1, 1).astype(BF16)

    @pl.loop(0, groups)
    def _(k):
        g = lax.rem(first + k, groups)
        row_copy(g).wait()
        part = at(g, group * cols)
        grow[:, part, :] = (prow[:, part, :] + precv[:, part, :]).astype(BF16)

    def finish(p):
        remote(up.at[:, at(p), :], U.at[me], su.at[p], ru.at[me], p).wait_send()
        remote(mloc.at[:, at(p), :], M.at[me], sm.at[p], rm.at[me], p).wait_send()
        remote(bloc.at[p], B.at[me], sb.at[p], rb.at[me], p).wait_send()

    each_peer(finish)


def fused_shards(n, tokens, upstream, row_factor, column_factor):
    _, rows, C, D = tokens.shape
    cols, R = C // n, rows * n
    full = R * cols
    group = 4
    groups = n // group
    vmem = pl.BlockSpec(memory_space=pltpu.VMEM)
    dma = pltpu.SemaphoreType.DMA
    grow, gcol = pl.pallas_call(
        functools.partial(kernel, n, group),
        out_shape=(
            jax.ShapeDtypeStruct((rows, C, C), BF16),
            jax.ShapeDtypeStruct((full, R), BF16),
        ),
        in_specs=[vmem] * 4,
        out_specs=(vmem, vmem),
        scratch_shapes=[
            pltpu.VMEM((n, rows, cols, D), BF16),
            pltpu.VMEM((n, rows, cols, D), BF16),
            pltpu.VMEM((rows, C, D), BF16),
            pltpu.VMEM((n, rows, cols, D), BF16),
            pltpu.VMEM((n, rows, cols, D), BF16),
            pltpu.VMEM((full, full), BF16),
            pltpu.VMEM((rows, C, C), F32),
            pltpu.VMEM((rows, C, C), F32),
            pltpu.VMEM((R, full), F32),
            pltpu.VMEM((R, full), F32),
        ] + [dma((n,))] * 6 + [dma((groups,))] * 2 + [dma, dma],
        compiler_params=pltpu.CompilerParams(
            collective_id=0, has_side_effects=True, vmem_limit_bytes=40 << 20
        ),
    )(tokens[0], upstream[0], row_factor, column_factor.reshape(full, R))
    return grow, gcol.reshape(cols, R, R)


def shards(n, m, tokens, upstream, row_factor, column_factor):
    docs, rows, C, D = tokens.shape
    cols, R = C // n, rows * n
    power = R & (R - 1) == 0 and cols & (cols - 1) == 0
    if m == 2 and docs == 1 and n % 4 == 0 and cols % 16 == 0 and D % 256 == 0 and power:
        return fused_shards(n, tokens, upstream, row_factor, column_factor)
    return plain_shards(tokens, upstream, row_factor, column_factor)


def solution(mesh):
    placed = (
        P("dp", "seq", None, None),
        P("dp", "seq", None, None),
        P("seq", None, None),
        P("seq", None, None),
    )
    return jax.shard_map(
        functools.partial(shards, mesh.shape["seq"], mesh.shape["dp"]),
        mesh=mesh,
        in_specs=placed,
        out_specs=(P("seq", None, None), P("seq", None, None)),
        check_vma=False,
    )
```

time: 104 us -> 74.1 us (0.71)
  the two profiles are of different devices: /device:TPU:0 before, /device:TPU:13 now
where the time goes in v1:
time: 74.1 us; the launch traced here: 73.9 us
  Pallas kernels  67.8 us (91%)
  local copies, waits for them, and re-layouts  5.47 us (7%)
    pallas_call x1, Pallas kernels, fused_shards(): pl.pallas_call(functools.partial(kernel, n, group), out_shape=(jax.ShapeD...  67.8 us
    unnamed x10, local copies, waits for them, and re-layouts  5.47 us

profile of v1, /device:TPU:13, one launch (start us, length us, event | category | flops | bytes accessed | tf_op | source)
XLA Modules:
  0.0 73.9 jit_solution(17131623571145906510)
XLA Ops:
  0.6 0.0 copy-start
  0.6 1.1 %copy-done = bf16[1,2,256,768]{3,2,1,0:T(8,128)(2,1)S(1)} copy-done((bf16[1,2,256,768]{3,2,1,0:T(8,128)(2,1)S(1)}, bf16[1,2,256,768]{3,2,1,0:T(8,128)(2,1)}, u32[]{:S(2)}) %copy-start) | copy-done | bytes 786456
  1.8 0.0 copy-start.1
  1.8 1.1 %copy-done.1 = bf16[1,2,256,768]{3,2,1,0:T(8,128)(2,1)S(1)} copy-done((bf16[1,2,256,768]{3,2,1,0:T(8,128)(2,1)S(1)}, bf16[1,2,256,768]{3,2,1,0:T(8,128)(2,1)}, u32[]{:S(2)}) %copy-start.1) | copy-done | bytes 786456
  2.9 0.0 copy-start.2
  2.9 0.9 %copy-done.2 = bf16[2,256,256]{2,1,0:T(8,128)(2,1)S(1)} copy-done((bf16[2,256,256]{2,1,0:T(8,128)(2,1)S(1)}, bf16[2,256,256]{2,1,0:T(8,128)(2,1)}, u32[]{:S(2)}) %copy-start.2) | copy-done | bytes 262168
  3.8 0.0 copy-start.3
  3.9 0.9 %copy-done.3 = bf16[16,32,32]{2,1,0:T(8,128)(2,1)S(1)} copy-done((bf16[16,32,32]{2,1,0:T(8,128)(2,1)S(1)}, bf16[16,32,32]{2,1,0:T(8,128)(2,1)}, u32[]{:S(2)}) %copy-start.3) | copy-done | bytes 32792
  4.8 67.8 %shard_map.59 = (bf16[2,256,256]{2,1,0:T(8,128)(2,1)S(1)}, bf16[512,32]{1,0:T(8,128)(2,1)S(1)}) custom-call(bf16[2,256,768]{2,1,0:T(8,128)(2,1)S(1)} %bitcast.4, bf16[2,256,768]{2,1,0:T(8,128)(2,1)S(1)} %bitcast.5, bf16[2,256,256]{2,1,0:T(8,128)(2,1)S(1)} %copy-done.2, bf16[512,32]{1,0:T(8,128)(2,1)S(1)} %bitcast.7), custom_call_target="tpu_custom_call" | custom-call | tf_op jit(solution)/shard_map/pallas_call | solution.py:168
  72.5 0.7 copy.8
  73.2 0.7 copy.9
Async XLA Ops:
  0.6 1.1 %copy-start = (bf16[1,2,256,768]{3,2,1,0:T(8,128)(2,1)S(1)}, bf16[1,2,256,768]{3,2,1,0:T(8,128)(2,1)}, u32[]{:S(2)}) copy-start(bf16[1,2,256,768]{3,2,1,0:T(8,128)(2,1)} %param.4) | copy-start | bytes 2359300
  1.8 1.1 %copy-start.1 = (bf16[1,2,256,768]{3,2,1,0:T(8,128)(2,1)S(1)}, bf16[1,2,256,768]{3,2,1,0:T(8,128)(2,1)}, u32[]{:S(2)}) copy-start(bf16[1,2,256,768]{3,2,1,0:T(8,128)(2,1)} %param.5) | copy-start | bytes 2359300
  2.9 0.9 %copy-start.2 = (bf16[2,256,256]{2,1,0:T(8,128)(2,1)S(1)}, bf16[2,256,256]{2,1,0:T(8,128)(2,1)}, u32[]{:S(2)}) copy-start(bf16[2,256,256]{2,1,0:T(8,128)(2,1)} %rf.1) | copy-start | bytes 786436
  3.8 0.9 %copy-start.3 = (bf16[16,32,32]{2,1,0:T(8,128)(2,1)S(1)}, bf16[16,32,32]{2,1,0:T(8,128)(2,1)}, u32[]{:S(2)}) copy-start(bf16[16,32,32]{2,1,0:T(8,128)(2,1)} %param.7) | copy-start | bytes 98308

commit v2 on v0

v2 whole, which is shorter than its diff:
```python
import functools

import jax
import jax.numpy as jnp
from jax import lax
from jax.experimental import pallas as pl
from jax.experimental.pallas import tpu as pltpu
from jax.sharding import PartitionSpec as P

F32, BF16 = jnp.float32, jnp.bfloat16


def apply_rows(row_factor, tokens):
    return jnp.einsum(
        "rij,brjd->brid", row_factor, tokens, preferred_element_type=F32
    ).astype(BF16)


def plain_shards(tokens, upstream, row_factor, column_factor):
    mixed = apply_rows(row_factor, tokens)
    mixed_cols, upstream_cols = (
        lax.all_to_all(mixed, "seq", split_axis=2, concat_axis=1, tiled=True),
        lax.all_to_all(upstream, "seq", split_axis=2, concat_axis=1, tiled=True),
    )
    sum_column = jnp.einsum(
        "brcd,bscd->crs", upstream_cols, mixed_cols, preferred_element_type=F32
    )
    back_cols = jnp.einsum(
        "crs,brcd->bscd", column_factor, upstream_cols, preferred_element_type=F32
    ).astype(BF16)
    back_rows = lax.all_to_all(back_cols, "seq", split_axis=1, concat_axis=2, tiled=True)
    sum_row = jnp.einsum("brid,brjd->rij", back_rows, tokens, preferred_element_type=F32)
    total_row, total_column = lax.psum((sum_row, sum_column), "dp")
    return (total_row.astype(BF16), total_column.astype(BF16))


def dot(a, b, ca=1, cb=0):
    return lax.dot_general(a, b, (((ca,), (cb,)), ((), ())), preferred_element_type=F32)


def kernel(n, outer_jobs, tok, up, rf, cf, grow, gcol,
           U, M, mloc, bloc, B, cfs, prow, precv, pcol, pcolr,
           su, ru, sf, sm, rm, sb, rb, sk, rk, sr, rr, sc, rc):
    me, doc = lax.axis_index("seq"), lax.axis_index("dp")
    other = 1 - doc
    rows, C, D = up.shape
    cols = C // n
    R = rows * n
    lc, lr = cols.bit_length() - 1, R.bit_length() - 1
    full, part_rows = R * cols, R * cols // 2
    layers, plane, half_n = 4, n // 4, n // 2
    inner_jobs = layers - outer_jobs
    half = lax.div(me, half_n)
    layer = lax.div(me, plane)
    outer = (layer == 0) | (layer == layers - 1)
    jobs = jnp.where(outer, outer_jobs, inner_jobs)
    first_k = jnp.where(outer, 0, outer_jobs)
    base = half * half_n
    MESH = pl.DeviceIdType.MESH

    def at(p, width=cols):
        return pl.ds(pl.multiple_of(p * width, width), width)

    def owner(h, j):
        k, place = lax.div(j, plane), lax.rem(j, plane)
        far = k < outer_jobs
        z = jnp.where(far, h * (layers - 1), 1 + h)
        return z * plane + place, jnp.where(far, k, k - outer_jobs)

    def chunk(slot):
        return (first_k + slot) * plane + lax.rem(me, plane)

    def remote(src, dst, send, recv, p, d=None):
        return pltpu.make_async_remote_copy(
            src_ref=src, dst_ref=dst, send_sem=send, recv_sem=recv,
            device_id={"dp": doc if d is None else d, "seq": p}, device_id_type=MESH)

    def greet(p, d):
        pl.semaphore_signal(barrier, inc=1, device_id={"dp": d, "seq": p}, device_id_type=MESH)

    barrier = pltpu.get_barrier_semaphore()

    @pl.loop(1, n)
    def _(k):
        greet(lax.rem(me + k, n), doc)

    greet(me, other)

    @pl.loop(0, jobs)
    def _(slot):
        greet(chunk(slot), other)

    for h in range(2):
        greet(owner(h, me)[0], other)
    pl.semaphore_wait(barrier, n + 2 + jobs)

    def u_copy(h, j):
        p, slot = owner(h, j)
        return p, remote(up.at[:, at(j), :], U.at[slot, me], su.at[h, j], ru.at[slot, me], p)

    def direct(h, j):
        return (h == half) | jnp.logical_not(outer) | (lax.div(j, plane) < outer_jobs)

    def f_copy(h):
        p, slot = owner(h, me)
        return p, remote(cf, cfs.at[slot], sk.at[h], rk.at[slot], p)

    @pl.loop(0, n)
    def _(j):
        for far in (1, 0):
            h = 1 - half if far else half
            p, copy = u_copy(h, j)

            @pl.when((p != me) & direct(h, j))
            def _():
                copy.start()

    for h in range(2):
        p, copy = f_copy(h)

        @pl.when(p != me)
        def _():
            copy.start()

        @pl.when(p == me)
        def _():
            cfs[owner(h, me)[1]] = cf[...]

    @pl.loop(0, jobs)
    def _(slot):
        U[slot, me] = up[:, at(chunk(slot)), :]

    for r in range(rows):
        for q in range(0, D, 256):
            mloc[r, :, q:q + 256] = dot(rf[r], tok[r, :, q:q + 256]).astype(BF16)

    def wait_u_sends():
        @pl.loop(0, n)
        def _(j):
            for h in range(2):
                p, copy = u_copy(h, j)

                @pl.when((p != me) & direct(h, j))
                def _():
                    copy.wait_send()

    @pl.when(outer)
    def _():
        wait_u_sends()

    def m_copy(j):
        p, slot = owner(half, j)
        src = me - base
        return p, remote(mloc.at[:, at(j), :], M.at[slot, src], sm.at[j], rm.at[slot, src], p)

    @pl.loop(0, n)
    def _(j):
        p, copy = m_copy(j)

        @pl.when(p != me)
        def _():
            copy.start()

    @pl.loop(0, jobs)
    def _(slot):
        M[slot, me - base] = mloc[:, at(chunk(slot)), :]

    def u_arrival(slot, src):
        return remote(U.at[slot, src], U.at[slot, src], sf.at[slot, lax.rem(src, plane)],
                      ru.at[slot, src], n - 1 - me + 2 * lax.rem(me, plane) - plane + 1)

    edge = half * (layers - 1) * plane

    @pl.when(jnp.logical_not(outer))
    def _():
        @pl.loop(0, inner_jobs)
        def _(slot):
            @pl.loop(0, plane)
            def _(q):
                copy = u_arrival(slot, edge + q)
                copy.wait_recv()
                copy.start()

    def iota(shape, dim):
        return lax.broadcasted_iota(jnp.int32, shape, dim)

    def ones(mask):
        return mask.astype(F32).astype(BF16)

    i, j = iota((full, full), 0), iota((full, full), 1)
    perm = ones(((i >> lr) == (j & (cols - 1))) & ((i & (R - 1)) == (j >> lc)))
    same = (iota((part_rows, full), 0) & (cols - 1)) == (iota((part_rows, full), 1) & (cols - 1))
    spread = ones((iota((part_rows, R), 0) >> lc) + half * (R // 2) == iota((part_rows, R), 1))
    gather = ones((iota((part_rows, R // 2), 0) >> lc) == iota((part_rows, R // 2), 1))

    def b_copy(slot, q):
        j = chunk(slot)
        return base + q, remote(bloc.at[slot, q], B.at[j], sb.at[slot, q], rb.at[j], base + q)

    def back(slot):
        @pl.when(slot < jobs)
        def _():
            j = chunk(slot)

            @pl.when((j != me))
            def _():
                remote(cf, cfs.at[slot], sk.at[0], rk.at[slot], lax.rem(me + 1, n)).wait_recv()

            turned = dot(cfs[slot], perm, 0, 0).astype(BF16)
            kmat = jnp.where(same, dot(spread, turned), 0.0).astype(BF16)

            @pl.loop(0, n)
            def _(src):
                handed = jnp.logical_not(outer) & (src >= edge) & (src < edge + plane)

                @pl.when((src != me) & jnp.logical_not(handed))
                def _():
                    u_arrival(slot, src).wait_recv()

            for q in range(0, D, 256):
                flat = U[slot, :, :, :, q:q + 256].reshape(full, 256)
                bloc[slot, :, :, :, q:q + 256] = dot(kmat, flat).astype(BF16).reshape(
                    half_n, rows, cols, 256)

            @pl.loop(0, half_n)
            def _(q):
                p, copy = b_copy(slot, q)

                @pl.when(p != me)
                def _():
                    copy.start()

            B[j] = bloc[slot, me - base]

    def s_copy(slot, d):
        return remote(pcol.at[slot], pcolr.at[half, doc], sc.at[slot, d], rc.at[half, doc],
                      chunk(slot), d)

    def here(slot, d):
        return (chunk(slot) == me) & (doc == d)

    def column(slot):
        @pl.when(slot < jobs)
        def _():
            @pl.loop(0, half_n)
            def _(src):
                @pl.when(base + src != me)
                def _():
                    remote(mloc.at[:, at(0), :], M.at[slot, src], sm.at[0], rm.at[slot, src],
                           lax.rem(me + 1, n)).wait_recv()

            pairs = dot(M[slot].reshape(part_rows, D), U[slot].reshape(full, D), 1, 1)
            pairs = jnp.where(same, pairs, 0.0)
            high = pairs.astype(BF16)
            low = pairs - high.astype(F32)
            mid = low.astype(BF16)
            rest = (low - mid.astype(F32)).astype(BF16)
            pcol[slot] = dot(gather, high, 0, 0) + dot(gather, mid, 0, 0) + dot(gather, rest, 0, 0)
            for d in range(2):
                @pl.when(jnp.logical_not(here(slot, d)))
                def _():
                    s_copy(slot, d).start()

                @pl.when(here(slot, d))
                def _():
                    pcolr[half, doc] = pcol[slot]

    def row_copy(k):
        part = at(k, plane * cols)
        return remote(prow.at[:, part, :], precv.at[:, part, :], sr.at[k], rr.at[k], me, other)

    def row(k):
        @pl.loop(0, plane)
        def _(q):
            j = k * plane + q
            p, _slot = owner(half, j)

            @pl.when(p != me)
            def _():
                remote(bloc.at[0, 0], B.at[j], sb.at[0, 0], rb.at[j], p).wait_recv()

        part = at(k, plane * cols)
        for r in range(rows):
            block = B[k * plane:(k + 1) * plane, r].reshape(plane * cols, D)
            prow[r, part, :] = dot(block, tok[r], 1, 1)
        row_copy(k).start()

    back(0)
    back(1)
    row(0)
    back(2)
    row(1)
    column(0)
    column(1)
    column(2)
    row(2)
    row(3)

    for h in range(2):
        for d in range(2):
            p, _slot = owner(h, me)

            @pl.when(jnp.logical_not((p == me) & (doc == d)))
            def _():
                remote(pcol.at[0], pcolr.at[h, d], sc.at[0, 0], rc.at[h, d],
                       lax.rem(me + 1, n)).wait_recv()

    total = jnp.concatenate([pcolr[0, 0] + pcolr[0, 1], pcolr[1, 0] + pcolr[1, 1]], axis=0)
    gcol[...] = dot(perm, total.astype(BF16), 1, 1).astype(BF16)

    for k in range(layers):
        row_copy(k).wait()
        part = pl.ds(k * plane * cols, plane * cols)
        grow[:, part, :] = (prow[:, part, :] + precv[:, part, :]).astype(BF16)

    @pl.when(jnp.logical_not(outer))
    def _():
        wait_u_sends()

        @pl.loop(0, inner_jobs)
        def _(slot):
            @pl.loop(0, plane)
            def _(q):
                u_arrival(slot, edge + q).wait_send()

    for h in range(2):
        p, copy = f_copy(h)

        @pl.when(p != me)
        def _():
            copy.wait_send()

    @pl.loop(0, n)
    def _(j):
        p, copy = m_copy(j)

        @pl.when(p != me)
        def _():
            copy.wait_send()

    @pl.loop(0, jobs)
    def _(slot):
        @pl.loop(0, half_n)
        def _(q):
            p, copy = b_copy(slot, q)

            @pl.when(p != me)
            def _():
                copy.wait_send()

        for d in range(2):
            @pl.when(jnp.logical_not(here(slot, d)))
            def _():
                s_copy(slot, d).wait_send()


def fused_shards(n, tokens, upstream, row_factor, column_factor):
    _, rows, C, D = tokens.shape
    cols, R = C // n, rows * n
    full = R * cols
    outer_jobs, slots = 1, 3
    vmem = pl.BlockSpec(memory_space=pltpu.VMEM)
    dma = pltpu.SemaphoreType.DMA
    grow, gcol = pl.pallas_call(
        functools.partial(kernel, n, outer_jobs),
        out_shape=(
            jax.ShapeDtypeStruct((rows, C, C), BF16),
            jax.ShapeDtypeStruct((full, R), BF16),
        ),
        in_specs=[vmem] * 4,
        out_specs=(vmem, vmem),
        scratch_shapes=[
            pltpu.VMEM((slots, n, rows, cols, D), BF16),
            pltpu.VMEM((slots, n // 2, rows, cols, D), BF16),
            pltpu.VMEM((rows, C, D), BF16),
            pltpu.VMEM((slots, n // 2, rows, cols, D), BF16),
            pltpu.VMEM((n, rows, cols, D), BF16),
            pltpu.VMEM((slots, full, R), BF16),
            pltpu.VMEM((rows, C, C), F32),
            pltpu.VMEM((rows, C, C), F32),
            pltpu.VMEM((slots, R // 2, full), F32),
            pltpu.VMEM((2, 2, R // 2, full), F32),
            dma((2, n)), dma((slots, n)), dma((slots, n // 4)),
            dma((n,)), dma((slots, n // 2)),
            dma((slots, n // 2)), dma((n,)),
            dma((2,)), dma((slots,)),
            dma((4,)), dma((4,)),
            dma((slots, 2)), dma((2, 2)),
        ],
        compiler_params=pltpu.CompilerParams(
            collective_id=0, has_side_effects=True, vmem_limit_bytes=48 << 20
        ),
    )(tokens[0], upstream[0], row_factor, column_factor.reshape(full, R))
    return grow, gcol.reshape(cols, R, R)


def shards(n, m, tokens, upstream, row_factor, column_factor):
    docs, rows, C, D = tokens.shape
    cols, R = C // n, rows * n
    power = R & (R - 1) == 0 and cols & (cols - 1) == 0
    if m == 2 and docs == 1 and n == 16 and cols % 16 == 0 and D % 256 == 0 and power:
        return fused_shards(n, tokens, upstream, row_factor, column_factor)
    return plain_shards(tokens, upstream, row_factor, column_factor)


def solution(mesh):
    placed = (
        P("dp", "seq", None, None),
        P("dp", "seq", None, None),
        P("seq", None, None),
        P("seq", None, None),
    )
    return jax.shard_map(
        functools.partial(shards, mesh.shape["seq"], mesh.shape["dp"]),
        mesh=mesh,
        in_specs=placed,
        out_specs=(P("seq", None, None), P("seq", None, None)),
        check_vma=False,
    )
```

time: 104 us -> 68.5 us (0.66)
  the two profiles are of different devices: /device:TPU:0 before, /device:TPU:20 now
where the time goes in v2:
time: 68.5 us; the launch traced here: 68.2 us
  Pallas kernels  62.1 us (91%)
  local copies, waits for them, and re-layouts  5.47 us (8%)
    pallas_call x1, Pallas kernels, fused_shards(): pl.pallas_call(functools.partial(kernel, n, outer_jobs), out_shape=(jax.S...  62.1 us
    unnamed x10, local copies, waits for them, and re-layouts  5.47 us

profile of v2, /device:TPU:20, one launch (start us, length us, event | category | flops | bytes accessed | tf_op | source)
XLA Modules:
  0.0 68.2 jit_solution(1540545122099855939)
XLA Ops:
  0.6 0.0 copy-start
  0.6 1.1 %copy-done = bf16[1,2,256,768]{3,2,1,0:T(8,128)(2,1)S(1)} copy-done((bf16[1,2,256,768]{3,2,1,0:T(8,128)(2,1)S(1)}, bf16[1,2,256,768]{3,2,1,0:T(8,128)(2,1)}, u32[]{:S(2)}) %copy-start) | copy-done | bytes 786456
  1.8 0.0 copy-start.1
  1.8 1.1 %copy-done.1 = bf16[1,2,256,768]{3,2,1,0:T(8,128)(2,1)S(1)} copy-done((bf16[1,2,256,768]{3,2,1,0:T(8,128)(2,1)S(1)}, bf16[1,2,256,768]{3,2,1,0:T(8,128)(2,1)}, u32[]{:S(2)}) %copy-start.1) | copy-done | bytes 786456
  2.9 0.0 copy-start.2
  2.9 0.9 %copy-done.2 = bf16[2,256,256]{2,1,0:T(8,128)(2,1)S(1)} copy-done((bf16[2,256,256]{2,1,0:T(8,128)(2,1)S(1)}, bf16[2,256,256]{2,1,0:T(8,128)(2,1)}, u32[]{:S(2)}) %copy-start.2) | copy-done | bytes 262168
  3.8 0.0 copy-start.3
  3.9 0.9 %copy-done.3 = bf16[16,32,32]{2,1,0:T(8,128)(2,1)S(1)} copy-done((bf16[16,32,32]{2,1,0:T(8,128)(2,1)S(1)}, bf16[16,32,32]{2,1,0:T(8,128)(2,1)}, u32[]{:S(2)}) %copy-start.3) | copy-done | bytes 32792
  4.8 62.1 %shard_map.59 = (bf16[2,256,256]{2,1,0:T(8,128)(2,1)S(1)}, bf16[512,32]{1,0:T(8,128)(2,1)S(1)}) custom-call(bf16[2,256,768]{2,1,0:T(8,128)(2,1)S(1)} %bitcast.4, bf16[2,256,768]{2,1,0:T(8,128)(2,1)S(1)} %bitcast.5, bf16[2,256,256]{2,1,0:T(8,128)(2,1)S(1)} %copy-done.2, bf16[512,32]{1,0:T(8,128)(2,1)S(1)} %bitcast.7), custom_call_target="tpu_custom_call" | custom-call | tf_op jit(solution)/shard_map/pallas_call | solution.py:364
  66.9 0.7 %copy.8 = bf16[2,256,256]{2,1,0:T(8,128)(2,1)} copy(bf16[2,256,256]{2,1,0:T(8,128)(2,1)S(1)} %get-tuple-element.8) | data formatting | bytes 524288
  67.6 0.7 copy.9
Async XLA Ops:
  0.6 1.1 %copy-start = (bf16[1,2,256,768]{3,2,1,0:T(8,128)(2,1)S(1)}, bf16[1,2,256,768]{3,2,1,0:T(8,128)(2,1)}, u32[]{:S(2)}) copy-start(bf16[1,2,256,768]{3,2,1,0:T(8,128)(2,1)} %param.4) | copy-start | bytes 2359300
  1.8 1.1 %copy-start.1 = (bf16[1,2,256,768]{3,2,1,0:T(8,128)(2,1)S(1)}, bf16[1,2,256,768]{3,2,1,0:T(8,128)(2,1)}, u32[]{:S(2)}) copy-start(bf16[1,2,256,768]{3,2,1,0:T(8,128)(2,1)} %param.5) | copy-start | bytes 2359300
  2.9 0.9 %copy-start.2 = (bf16[2,256,256]{2,1,0:T(8,128)(2,1)S(1)}, bf16[2,256,256]{2,1,0:T(8,128)(2,1)}, u32[]{:S(2)}) copy-start(bf16[2,256,256]{2,1,0:T(8,128)(2,1)} %rf.1) | copy-start | bytes 786436
  3.8 0.9 %copy-start.3 = (bf16[16,32,32]{2,1,0:T(8,128)(2,1)S(1)}, bf16[16,32,32]{2,1,0:T(8,128)(2,1)}, u32[]{:S(2)}) copy-start(bf16[16,32,32]{2,1,0:T(8,128)(2,1)} %param.7) | copy-start | bytes 98308

commit v3 on v2

--- a/solution.py
+++ b/solution.py
@@ -282,7 +282,7 @@
         part = at(k, plane * cols)
         for r in range(rows):
             block = B[k * plane:(k + 1) * plane, r].reshape(plane * cols, D)
-            prow[r, part, :] = dot(block, tok[r], 1, 1)
+            prow[r, part, :] = dot(block, tok[r], 1, 1).astype(BF16)
         row_copy(k).start()
 
     back(0)
@@ -311,7 +311,7 @@
     for k in range(layers):
         row_copy(k).wait()
         part = pl.ds(k * plane * cols, plane * cols)
-        grow[:, part, :] = (prow[:, part, :] + precv[:, part, :]).astype(BF16)
+        grow[:, part, :] = (prow[:, part, :].astype(F32) + precv[:, part, :].astype(F32)).astype(BF16)
 
     @pl.when(jnp.logical_not(outer))
     def _():
@@ -376,8 +376,8 @@
             pltpu.VMEM((slots, n // 2, rows, cols, D), BF16),
             pltpu.VMEM((n, rows, cols, D), BF16),
             pltpu.VMEM((slots, full, R), BF16),
-            pltpu.VMEM((rows, C, C), F32),
-            pltpu.VMEM((rows, C, C), F32),
+            pltpu.VMEM((rows, C, C), BF16),
+            pltpu.VMEM((rows, C, C), BF16),
             pltpu.VMEM((slots, R // 2, full), F32),
             pltpu.VMEM((2, 2, R // 2, full), F32),
             dma((2, n)), dma((slots, n)), dma((slots, n // 4)),

time: 68.5 us -> 65.9 us (0.962)
  the two profiles are of different devices: /device:TPU:20 before, /device:TPU:0 now
where the time goes in v3:
time: 65.9 us; the launch traced here: 65.6 us
  Pallas kernels  59.5 us (90%)
  local copies, waits for them, and re-layouts  5.47 us (8%)
    pallas_call x1, Pallas kernels, fused_shards(): pl.pallas_call(functools.partial(kernel, n, outer_jobs), out_shape=(jax.S...  59.5 us
    unnamed x10, local copies, waits for them, and re-layouts  5.47 us

profile of v3, /device:TPU:0, one launch (start us, length us, event | category | flops | bytes accessed | tf_op | source)
XLA Modules:
  0.0 65.6 jit_solution(16655847782587056293)
XLA Ops:
  0.6 0.0 copy-start
  0.6 1.1 %copy-done = bf16[1,2,256,768]{3,2,1,0:T(8,128)(2,1)S(1)} copy-done((bf16[1,2,256,768]{3,2,1,0:T(8,128)(2,1)S(1)}, bf16[1,2,256,768]{3,2,1,0:T(8,128)(2,1)}, u32[]{:S(2)}) %copy-start) | copy-done | bytes 786456
  1.8 0.0 copy-start.1
  1.8 1.1 %copy-done.1 = bf16[1,2,256,768]{3,2,1,0:T(8,128)(2,1)S(1)} copy-done((bf16[1,2,256,768]{3,2,1,0:T(8,128)(2,1)S(1)}, bf16[1,2,256,768]{3,2,1,0:T(8,128)(2,1)}, u32[]{:S(2)}) %copy-start.1) | copy-done | bytes 786456
  2.9 0.0 copy-start.2
  2.9 0.9 %copy-done.2 = bf16[2,256,256]{2,1,0:T(8,128)(2,1)S(1)} copy-done((bf16[2,256,256]{2,1,0:T(8,128)(2,1)S(1)}, bf16[2,256,256]{2,1,0:T(8,128)(2,1)}, u32[]{:S(2)}) %copy-start.2) | copy-done | bytes 262168
  3.8 0.0 copy-start.3
  3.9 0.9 %copy-done.3 = bf16[16,32,32]{2,1,0:T(8,128)(2,1)S(1)} copy-done((bf16[16,32,32]{2,1,0:T(8,128)(2,1)S(1)}, bf16[16,32,32]{2,1,0:T(8,128)(2,1)}, u32[]{:S(2)}) %copy-start.3) | copy-done | bytes 32792
  4.8 59.5 %shard_map.59 = (bf16[2,256,256]{2,1,0:T(8,128)(2,1)S(1)}, bf16[512,32]{1,0:T(8,128)(2,1)S(1)}) custom-call(bf16[2,256,768]{2,1,0:T(8,128)(2,1)S(1)} %bitcast.4, bf16[2,256,768]{2,1,0:T(8,128)(2,1)S(1)} %bitcast.5, bf16[2,256,256]{2,1,0:T(8,128)(2,1)S(1)} %copy-done.2, bf16[512,32]{1,0:T(8,128)(2,1)S(1)} %bitcast.7), custom_call_target="tpu_custom_call" | custom-call | tf_op jit(solution)/shard_map/pallas_call | solution.py:364
  64.3 0.7 %copy.8 = bf16[2,256,256]{2,1,0:T(8,128)(2,1)} copy(bf16[2,256,256]{2,1,0:T(8,128)(2,1)S(1)} %get-tuple-element.8) | data formatting | bytes 524288
  65.0 0.7 copy.9
Async XLA Ops:
  0.6 1.1 %copy-start = (bf16[1,2,256,768]{3,2,1,0:T(8,128)(2,1)S(1)}, bf16[1,2,256,768]{3,2,1,0:T(8,128)(2,1)}, u32[]{:S(2)}) copy-start(bf16[1,2,256,768]{3,2,1,0:T(8,128)(2,1)} %param.4) | copy-start | bytes 2359300
  1.8 1.1 %copy-start.1 = (bf16[1,2,256,768]{3,2,1,0:T(8,128)(2,1)S(1)}, bf16[1,2,256,768]{3,2,1,0:T(8,128)(2,1)}, u32[]{:S(2)}) copy-start(bf16[1,2,256,768]{3,2,1,0:T(8,128)(2,1)} %param.5) | copy-start | bytes 2359300
  2.9 0.9 %copy-start.2 = (bf16[2,256,256]{2,1,0:T(8,128)(2,1)S(1)}, bf16[2,256,256]{2,1,0:T(8,128)(2,1)}, u32[]{:S(2)}) copy-start(bf16[2,256,256]{2,1,0:T(8,128)(2,1)} %rf.1) | copy-start | bytes 786436
  3.8 0.9 %copy-start.3 = (bf16[16,32,32]{2,1,0:T(8,128)(2,1)S(1)}, bf16[16,32,32]{2,1,0:T(8,128)(2,1)}, u32[]{:S(2)}) copy-start(bf16[16,32,32]{2,1,0:T(8,128)(2,1)} %param.7) | copy-start | bytes 98308

commit v4 on v3

--- a/solution.py
+++ b/solution.py
@@ -70,6 +70,9 @@
     def chunk(slot):
         return (first_k + slot) * plane + lax.rem(me, plane)
 
+    def turn(step):
+        return lax.div(step, plane) * plane + lax.rem(me + step, plane)
+
     def remote(src, dst, send, recv, p, d=None):
         return pltpu.make_async_remote_copy(
             src_ref=src, dst_ref=dst, send_sem=send, recv_sem=recv,
@@ -106,7 +109,8 @@
         return p, remote(cf, cfs.at[slot], sk.at[h], rk.at[slot], p)
 
     @pl.loop(0, n)
-    def _(j):
+    def _(step):
+        j = turn(step)
         for far in (1, 0):
             h = 1 - half if far else half
             p, copy = u_copy(h, j)
@@ -154,8 +158,8 @@
         return p, remote(mloc.at[:, at(j), :], M.at[slot, src], sm.at[j], rm.at[slot, src], p)
 
     @pl.loop(0, n)
-    def _(j):
-        p, copy = m_copy(j)
+    def _(step):
+        p, copy = m_copy(turn(step))
 
         @pl.when(p != me)
         def _():
@@ -223,8 +227,8 @@
                     half_n, rows, cols, 256)
 
             @pl.loop(0, half_n)
-            def _(q):
-                p, copy = b_copy(slot, q)
+            def _(step):
+                p, copy = b_copy(slot, lax.rem(me + step, half_n))
 
                 @pl.when(p != me)
                 def _():

time: 65.9 us -> 65.3 us (level)
  Pallas kernels: 59.5 us -> 58.7 us
    pallas_call x1, Pallas kernels: 59.5 us -> 58.7 us  [fused_shards(): pl.pallas_call(functools.partial(kernel, n, outer_jobs), out_shape=(jax.S...]
where the time goes in v4:
time: 65.3 us; the launch traced here: 64.8 us
  Pallas kernels  58.7 us (90%)
  local copies, waits for them, and re-layouts  5.47 us (8%)
    pallas_call x1, Pallas kernels, fused_shards(): pl.pallas_call(functools.partial(kernel, n, outer_jobs), out_shape=(jax.S...  58.7 us
    unnamed x10, local copies, waits for them, and re-layouts  5.47 us

profile of v4, /device:TPU:0, one launch (start us, length us, event | category | flops | bytes accessed | tf_op | source)
XLA Modules:
  0.0 64.8 jit_solution(4190485350944696609)
XLA Ops:
  0.6 0.0 copy-start
  0.6 1.1 %copy-done = bf16[1,2,256,768]{3,2,1,0:T(8,128)(2,1)S(1)} copy-done((bf16[1,2,256,768]{3,2,1,0:T(8,128)(2,1)S(1)}, bf16[1,2,256,768]{3,2,1,0:T(8,128)(2,1)}, u32[]{:S(2)}) %copy-start) | copy-done | bytes 786456
  1.8 0.0 copy-start.1
  1.8 1.1 %copy-done.1 = bf16[1,2,256,768]{3,2,1,0:T(8,128)(2,1)S(1)} copy-done((bf16[1,2,256,768]{3,2,1,0:T(8,128)(2,1)S(1)}, bf16[1,2,256,768]{3,2,1,0:T(8,128)(2,1)}, u32[]{:S(2)}) %copy-start.1) | copy-done | bytes 786456
  2.9 0.0 copy-start.2
  2.9 0.9 %copy-done.2 = bf16[2,256,256]{2,1,0:T(8,128)(2,1)S(1)} copy-done((bf16[2,256,256]{2,1,0:T(8,128)(2,1)S(1)}, bf16[2,256,256]{2,1,0:T(8,128)(2,1)}, u32[]{:S(2)}) %copy-start.2) | copy-done | bytes 262168
  3.8 0.0 copy-start.3
  3.9 0.9 %copy-done.3 = bf16[16,32,32]{2,1,0:T(8,128)(2,1)S(1)} copy-done((bf16[16,32,32]{2,1,0:T(8,128)(2,1)S(1)}, bf16[16,32,32]{2,1,0:T(8,128)(2,1)}, u32[]{:S(2)}) %copy-start.3) | copy-done | bytes 32792
  4.8 58.7 %shard_map.59 = (bf16[2,256,256]{2,1,0:T(8,128)(2,1)S(1)}, bf16[512,32]{1,0:T(8,128)(2,1)S(1)}) custom-call(bf16[2,256,768]{2,1,0:T(8,128)(2,1)S(1)} %bitcast.4, bf16[2,256,768]{2,1,0:T(8,128)(2,1)S(1)} %bitcast.5, bf16[2,256,256]{2,1,0:T(8,128)(2,1)S(1)} %copy-done.2, bf16[512,32]{1,0:T(8,128)(2,1)S(1)} %bitcast.7), custom_call_target="tpu_custom_call" | custom-call | tf_op jit(solution)/shard_map/pallas_call | solution.py:368
  63.4 0.7 %copy.8 = bf16[2,256,256]{2,1,0:T(8,128)(2,1)} copy(bf16[2,256,256]{2,1,0:T(8,128)(2,1)S(1)} %get-tuple-element.8) | data formatting | bytes 524288
  64.1 0.7 %copy.9 = bf16[16,32,32]{2,1,0:T(8,128)(2,1)} copy(bf16[16,32,32]{2,1,0:T(8,128)(2,1)S(1)} %bitcast.6) | data formatting | bytes 65536
Async XLA Ops:
  0.6 1.1 %copy-start = (bf16[1,2,256,768]{3,2,1,0:T(8,128)(2,1)S(1)}, bf16[1,2,256,768]{3,2,1,0:T(8,128)(2,1)}, u32[]{:S(2)}) copy-start(bf16[1,2,256,768]{3,2,1,0:T(8,128)(2,1)} %param.4) | copy-start | bytes 2359300
  1.8 1.1 %copy-start.1 = (bf16[1,2,256,768]{3,2,1,0:T(8,128)(2,1)S(1)}, bf16[1,2,256,768]{3,2,1,0:T(8,128)(2,1)}, u32[]{:S(2)}) copy-start(bf16[1,2,256,768]{3,2,1,0:T(8,128)(2,1)} %param.5) | copy-start | bytes 2359300
  2.9 0.9 %copy-start.2 = (bf16[2,256,256]{2,1,0:T(8,128)(2,1)S(1)}, bf16[2,256,256]{2,1,0:T(8,128)(2,1)}, u32[]{:S(2)}) copy-start(bf16[2,256,256]{2,1,0:T(8,128)(2,1)} %rf.1) | copy-start | bytes 786436
  3.8 0.9 %copy-start.3 = (bf16[16,32,32]{2,1,0:T(8,128)(2,1)S(1)}, bf16[16,32,32]{2,1,0:T(8,128)(2,1)}, u32[]{:S(2)}) copy-start(bf16[16,32,32]{2,1,0:T(8,128)(2,1)} %param.7) | copy-start | bytes 98308
